TPU v7x, 32 devices: a whole 2x2x4 slice. The times are simulated.
32 devices in a mesh: section: 8 (over z, y), tile: 4 (over x, core).
Axes of the slice: x: 2, y: 2, z: 4, core: 2. Of those that a mesh axis runs over, the one named last changes fastest.
Arguments:
- acts: bfloat16 [8, 2, 256, 32, 128], P('section', None, None, 'tile'), may hold values from -6 to 6
- weights: bfloat16 [8, 9, 256, 256], P('section'), may hold values from -0.0625 to 0.0625
- cotangent: bfloat16 [2, 256, 32, 128], P(None, None, 'tile'), may hold values from -6 to 6
Outputs:
- grad_acts: bfloat16 [8, 2, 256, 32, 128], P('section', None, None, 'tile')
- weight_grad: float32 [8, 9, 256, 256], P('section')
All inputs are finite; a program needn't handle non-finite values.
Results may differ from a plain program's by a relative error of at most 0.017.
Values may be sent and summed in bfloat16 or wider, within the bound.
A program may use at most 64 MiB of HBM per device.

v0:
```python
import jax
import jax.numpy as jnp
from jax import lax
from jax.sharding import PartitionSpec as P


def padded_2(block, sides, width):
    for axis, dim in sides:
        count = lax.axis_size(axis)
        forward = [(i, i + 1) for i in range(count - 1)]
        forward.append((count - 1, 0))
        backward = [(target, source) for source, target in forward]
        low = lax.ppermute(
            lax.slice_in_dim(block, block.shape[dim] - width, None, axis=dim), axis, forward
        )
        high = lax.ppermute(lax.slice_in_dim(block, 0, width, axis=dim), axis, backward)
        block = jnp.concatenate([low, block, high], axis=dim)
    return block


def from_behind(block, axis, distance):
    devices = range(lax.axis_size(axis))
    route = [(i - distance, i) for i in devices if i - distance in devices]
    return lax.ppermute(block, axis, route)


def shift_cols(field, offset):
    if offset == 0:
        return field
    zeros = jnp.zeros_like(field[..., :1])
    if offset == 1:
        return jnp.concatenate([field[..., 1:], zeros], axis=-1)
    return jnp.concatenate([zeros, field[..., :-1]], axis=-1)


def back_conv(padded, kernel, height):
    total = jnp.zeros(padded.shape[:2] + (height, padded.shape[3]), jnp.float32)
    for row_step in (-1, 0, 1):
        rows_cut = padded[:, :, 1 - row_step : 1 - row_step + height, :]
        for col_step in (-1, 0, 1):
            index = (row_step + 1) * 3 + col_step + 1
            moved = shift_cols(rows_cut, -col_step)
            total = total + jnp.einsum(
                "oi,gorc->girc", kernel[index], moved, preferred_element_type=jnp.float32
            )
    return total


def kernel_grad(padded, hidden_rims, height):
    grad_mid = padded[:, :, 1 : 1 + height, :]
    parts = []
    for row_step in (-1, 0, 1):
        rows_cut = hidden_rims[:, :, 1 + row_step : 1 + row_step + height, :]
        for col_step in (-1, 0, 1):
            seen = shift_cols(rows_cut, col_step)
            parts.append(
                jnp.einsum("gorc,girc->oi", grad_mid, seen, preferred_element_type=jnp.float32)
            )
    return jnp.stack(parts)


def per_device(acts, weights, cotangent):
    n_section = lax.axis_size("section")
    section_id = lax.axis_index("section")
    inputs = acts[0].astype(jnp.float32)
    kernel = weights[0]
    batches, chans, height, width = acts.shape[1:]
    sigma = jax.nn.sigmoid(inputs)
    hidden = (inputs * sigma).astype(jnp.bfloat16)
    slope = sigma * (1.0 + inputs * (1.0 - sigma))
    hidden_rims = padded_2(hidden, (("tile", 2),), 1)
    scale = 1.0 / jnp.sqrt(jnp.float32(batches * height * lax.axis_size("tile") * width))
    n_groups = batches // batches
    ticks = n_section + n_groups - 1

    def one_tick(carry, tick):
        incoming, grads, kernel_acc, stored = carry
        batch_id = tick - (n_section - 1 - section_id)
        valid = jnp.logical_and(batch_id >= 0, batch_id < n_groups)
        upper = jnp.where(section_id == n_section - 1, cotangent, incoming)
        padded = padded_2(upper, (("tile", 2),), 1)

        def active(operands):
            padded_in, upper_in, slope_in, rims_in = operands
            back = back_conv(padded_in, kernel, height)
            lowered = (upper_in.astype(jnp.float32) + back * slope_in).astype(jnp.bfloat16)
            partial_k = kernel_grad(padded_in, rims_in, height)
            return (lowered, partial_k)

        def resting(operands):
            return (jnp.zeros(upper.shape, jnp.bfloat16), jnp.zeros(kernel_acc.shape, jnp.float32))

        lowered, partial_k = lax.cond(valid, active, resting, (padded, upper, slope, hidden_rims))
        kernel_acc = kernel_acc + partial_k
        old_grads = grads
        grads = jnp.where(valid, lowered, old_grads)
        old_store = stored
        stored = jnp.where(valid, padded, old_store)
        outgoing = from_behind(lowered, "section", -1)
        return ((outgoing, grads, kernel_acc, stored), None)

    initial = (
        jnp.zeros((batches, chans, height, width), jnp.bfloat16),
        jnp.zeros((batches, chans, height, width), jnp.bfloat16),
        jnp.zeros((9, chans, chans), jnp.float32),
        jnp.zeros((batches, chans, height + 2, width), jnp.bfloat16),
    )
    final, unused = lax.scan(one_tick, initial, jnp.arange(ticks, dtype=jnp.int32))
    grads = final[1]
    kernel_acc = final[2]
    weight_grad = lax.psum(kernel_acc * scale, "tile")
    return (grads[None], weight_grad[None])


def solution(mesh):
    placed = (
        P("section", None, None, "tile", None),
        P("section", None, None, None),
        P(None, None, "tile", None),
    )
    return jax.shard_map(
        per_device,
        mesh=mesh,
        in_specs=placed,
        out_specs=(P("section", None, None, "tile", None), P("section", None, None, None)),
        check_vma=False,
    )
```

profile of v0, /device:TPU:0, one launch (start us, length us, event | category | flops | bytes accessed | tf_op | source)
XLA Modules:
  0.0 545.1 jit_solution(5333695063645161396)
XLA Ops:
  7.2 3.6 fusion.66
  14.8 2.9 copy.19
  18.9 460.3 %while.17 = (s32[]{:T(128)}, bf16[2,256,8,128]{1,3,2,0:T(8,128)(2,1)}, bf16[2,256,8,128]{1,3,2,0:T(8,128)(2,1)}, f32[9,256,256]{1,2,0:T(8,128)}, s32[8]{0:T(128)...) while((s32[]{:T(128)}, ...), condition=%wide.region_3.4_spmd.clone, body=%wide.region_0.3_spmd.clone.sunk | while | flops 4842192896 | bytes 153502240 | solution.py:108
  23.8 2.8 collective-permute-done
  29.0 2.7 conditional.3
  37.5 20.8 %collective-permute-done.2 = bf16[2,256,8,128]{1,3,2,0:T(8,128)(2,1)S(1)} collective-permute-done((bf16[2,256,8,128]{1,3,2,0:T(8,128)(2,1)}, bf16[2,256,8,128]{1,3,2,0:T(8,128)(2,1)S(1)}, u32[]{:S(2)}, u32[]{:S(2)}) %collective-permute-start.2) | collective-permute-done | bytes 1048608 | tf_op jit(solution)/shard_map/while/body/eval_jaxpr/ppermute | solution.py:24
  68.9 2.7 conditional.3
  72.9 2.5 select_select_fusion.2
  75.4 2.4 select_add_fusion.2
  77.9 21.0 %collective-permute-done.2 = bf16[2,256,8,128]{1,3,2,0:T(8,128)(2,1)S(1)} collective-permute-done((bf16[2,256,8,128]{1,3,2,0:T(8,128)(2,1)}, bf16[2,256,8,128]{1,3,2,0:T(8,128)(2,1)S(1)}, u32[]{:S(2)}, u32[]{:S(2)}) %collective-permute-start.2) | collective-permute-done | bytes 1048608 | tf_op jit(solution)/shard_map/while/body/eval_jaxpr/ppermute | solution.py:24
  108.7 2.7 conditional.3
  112.7 2.5 select_select_fusion.2
  117.6 20.9 %collective-permute-done.2 = bf16[2,256,8,128]{1,3,2,0:T(8,128)(2,1)S(1)} collective-permute-done((bf16[2,256,8,128]{1,3,2,0:T(8,128)(2,1)}, bf16[2,256,8,128]{1,3,2,0:T(8,128)(2,1)S(1)}, u32[]{:S(2)}, u32[]{:S(2)}) %collective-permute-start.2) | collective-permute-done | bytes 1048608 | tf_op jit(solution)/shard_map/while/body/eval_jaxpr/ppermute | solution.py:24
  143.9 2.6 collective-permute-done
  149.3 2.7 conditional.3
  153.3 2.5 select_select_fusion.2
  158.3 21.7 %collective-permute-done.2 = bf16[2,256,8,128]{1,3,2,0:T(8,128)(2,1)S(1)} collective-permute-done((bf16[2,256,8,128]{1,3,2,0:T(8,128)(2,1)}, bf16[2,256,8,128]{1,3,2,0:T(8,128)(2,1)S(1)}, u32[]{:S(2)}, u32[]{:S(2)}) %collective-permute-start.2) | collective-permute-done | bytes 1048608 | tf_op jit(solution)/shard_map/while/body/eval_jaxpr/ppermute | solution.py:24
  189.7 2.7 conditional.3
  193.7 2.5 select_select_fusion.2
  198.6 20.8 %collective-permute-done.2 = bf16[2,256,8,128]{1,3,2,0:T(8,128)(2,1)S(1)} collective-permute-done((bf16[2,256,8,128]{1,3,2,0:T(8,128)(2,1)}, bf16[2,256,8,128]{1,3,2,0:T(8,128)(2,1)S(1)}, u32[]{:S(2)}, u32[]{:S(2)}) %collective-permute-start.2) | collective-permute-done | bytes 1048608 | tf_op jit(solution)/shard_map/while/body/eval_jaxpr/ppermute | solution.py:24
  225.0 2.6 collective-permute-done
  230.3 2.7 conditional.3
  234.3 2.5 select_select_fusion.2
  239.3 21.6 %collective-permute-done.2 = bf16[2,256,8,128]{1,3,2,0:T(8,128)(2,1)S(1)} collective-permute-done((bf16[2,256,8,128]{1,3,2,0:T(8,128)(2,1)}, bf16[2,256,8,128]{1,3,2,0:T(8,128)(2,1)S(1)}, u32[]{:S(2)}, u32[]{:S(2)}) %collective-permute-start.2) | collective-permute-done | bytes 1048608 | tf_op jit(solution)/shard_map/while/body/eval_jaxpr/ppermute | solution.py:24
  270.6 2.7 conditional.3
  274.6 2.5 select_select_fusion.2
  279.6 140.7 %collective-permute-done.2 = bf16[2,256,8,128]{1,3,2,0:T(8,128)(2,1)S(1)} collective-permute-done((bf16[2,256,8,128]{1,3,2,0:T(8,128)(2,1)}, bf16[2,256,8,128]{1,3,2,0:T(8,128)(2,1)S(1)}, u32[]{:S(2)}, u32[]{:S(2)}) %collective-permute-start.2) | collective-permute-done | bytes 1048608 | tf_op jit(solution)/shard_map/while/body/eval_jaxpr/ppermute | solution.py:24
  430.3 20.9 %conditional.3 = (bf16[2,256,8,128]{1,3,2,0:T(8,128)(2,1)}, f32[9,256,256]{1,2,0:T(8,128)}) conditional(s32[]{:T(128)} %convert_element_type.29, () %tuple.63, (bf16[2,256,8,128]{1,3,2,0:T(8,128)(2,1)S(1)}, bf16[2,256,10,128]{1,3,2,0:T(8,128)(2,1)S(1)}, bf16[9,256,256]{2,1,0:T(8,128)(2,1)}, f32[2,256,8,128]{1,3,2,0:T(8,128)S(1)}, ...), branch_computations={%region_1.1_spmd, %region_2.2_spmd} | conditional | flops 4838129664 | bytes 100286512 | solution.py:93
  452.5 2.8 select_select_fusion.2
  457.8 20.4 %collective-permute-done.2 = bf16[2,256,8,128]{1,3,2,0:T(8,128)(2,1)S(1)} collective-permute-done((bf16[2,256,8,128]{1,3,2,0:T(8,128)(2,1)}, bf16[2,256,8,128]{1,3,2,0:T(8,128)(2,1)S(1)}, u32[]{:S(2)}, u32[]{:S(2)}) %collective-permute-start.2) | collective-permute-done | bytes 1048608 | tf_op jit(solution)/shard_map/while/body/eval_jaxpr/ppermute | solution.py:24
  485.5 49.5 %all-reduce.14.cloned.1.call-done = f32[1,9,256,256]{3,2,1,0:T(8,128)} async-done(((f32[1,9,256,256]{3,2,1,0:T(8,128)}), f32[1,9,256,256]{3,2,1,0:T(8,128)}) %all-reduce.14.cloned.1.call-update) | async-done | bytes 2359312 | tf_op jit(solution)/shard_map/psum | solution.py:111
  535.0 3.2 copy.79
  (197 shorter events, 149.8 us)
Async XLA Ops:
  7.2 527.9 %all-reduce.14.cloned.1.call-start = ((), (), s32[]{:S(2)}) async-start(), calls=%async_computation | async-start | bytes 4718592 | tf_op jit(solution)/shard_map/psum | solution.py:111
  10.8 6.9 %collective-permute-start.3 = (bf16[2,256,1,128]{3,1,2,0:T(8,128)(2,1)S(1)}, bf16[2,256,1,128]{3,1,2,0:T(8,128)(2,1)S(1)}, u32[]{:S(2)}, u32[]{:S(2)}) collective-permute-start(bf16[2,256,1,128]{3,1,2,0:T(8,128)(2,1)S(1)} %get-tuple-element.252), channel_id=1, source_target_pairs={{0,1},{1,2},{2,3},{3,0},{4,5},{5,6},{6,7},{7,4},{8,9},{9,10},{10,1... | collective-permute-start | bytes 393224 | tf_op jit(solution)/shard_map/ppermute | solution.py:13
  11.3 6.4 %collective-permute-start.4 = (bf16[2,256,1,128]{3,1,2,0:T(8,128)(2,1)S(1)}, bf16[2,256,1,128]{3,1,2,0:T(8,128)(2,1)S(1)}, u32[]{:S(2)}, u32[]{:S(2)}) collective-permute-start(bf16[2,256,1,128]{3,1,2,0:T(8,128)(2,1)S(1)} %get-tuple-element.253), channel_id=1, source_target_pairs={{1,0},{2,1},{3,2},{0,3},{5,4},{6,5},{7,6},{4,7},{9,8},{10,9},{11,1... | collective-permute-start | bytes 393224 | tf_op jit(solution)/shard_map/ppermute | solution.py:16
  21.0 5.6 %collective-permute-start = (bf16[2,256,1,128]{1,3,2,0:T(8,128)(2,1)}, bf16[2,256,1,128]{1,3,2,0:T(8,128)(2,1)S(1)}, u32[]{:S(2)}, u32[]{:S(2)}) collective-permute-start(bf16[2,256,1,128]{1,3,2,0:T(8,128)(2,1)} %get-tuple-element.333), channel_id=1, source_target_pairs={{1,0},{2,1},{3,2},{0,3},{5,4},{6,5},{7,6},{4,7},{9,8},{10,9},{11,1... | collective-permute-start | bytes 393224 | tf_op jit(solution)/shard_map/while/body/eval_jaxpr/ppermute | solution.py:16
  22.5 5.4 collective-permute-start.1
  31.7 26.6 %collective-permute-start.2 = (bf16[2,256,8,128]{1,3,2,0:T(8,128)(2,1)}, bf16[2,256,8,128]{1,3,2,0:T(8,128)(2,1)S(1)}, u32[]{:S(2)}, u32[]{:S(2)}) collective-permute-start(bf16[2,256,8,128]{1,3,2,0:T(8,128)(2,1)} %get-tuple-element.335), channel_id=1, source_target_pairs={{4,0},{8,4},{12,8},{16,12},{20,16},{24,20},{28,24},{5,1},{9,5},{13... | collective-permute-start | bytes 3145736 | tf_op jit(solution)/shard_map/while/body/eval_jaxpr/ppermute | solution.py:24
  61.3 4.2 collective-permute-start
  61.9 5.9 %collective-permute-start.1 = (bf16[2,256,1,128]{1,3,2,0:T(8,128)(2,1)}, bf16[2,256,1,128]{1,3,2,0:T(8,128)(2,1)}, u32[]{:S(2)}, u32[]{:S(2)}) collective-permute-start(bf16[2,256,1,128]{1,3,2,0:T(8,128)(2,1)} %get-tuple-element.334), channel_id=1, source_target_pairs={{0,1},{1,2},{2,3},{3,0},{4,5},{5,6},{6,7},{7,4},{8,9},{9,10},{10,1... | collective-permute-start | bytes 393224 | tf_op jit(solution)/shard_map/while/body/eval_jaxpr/ppermute | solution.py:13
  71.6 27.3 %collective-permute-start.2 = (bf16[2,256,8,128]{1,3,2,0:T(8,128)(2,1)}, bf16[2,256,8,128]{1,3,2,0:T(8,128)(2,1)S(1)}, u32[]{:S(2)}, u32[]{:S(2)}) collective-permute-start(bf16[2,256,8,128]{1,3,2,0:T(8,128)(2,1)} %get-tuple-element.335), channel_id=1, source_target_pairs={{4,0},{8,4},{12,8},{16,12},{20,16},{24,20},{28,24},{5,1},{9,5},{13... | collective-permute-start | bytes 3145736 | tf_op jit(solution)/shard_map/while/body/eval_jaxpr/ppermute | solution.py:24
  77.9 21.1 %copy-start.1 = (f32[9,256,256]{1,2,0:T(8,128)}, f32[9,256,256]{1,2,0:T(8,128)S(1)}, u32[]{:S(2)}) copy-start(f32[9,256,256]{1,2,0:T(8,128)S(1)} %select_add_fusion.2) | copy-start | bytes 7077892 | tf_op jit(solution)/shard_map/while
  102.0 3.9 collective-permute-start
  102.0 5.6 %collective-permute-start.1 = (bf16[2,256,1,128]{1,3,2,0:T(8,128)(2,1)}, bf16[2,256,1,128]{1,3,2,0:T(8,128)(2,1)}, u32[]{:S(2)}, u32[]{:S(2)}) collective-permute-start(bf16[2,256,1,128]{1,3,2,0:T(8,128)(2,1)} %get-tuple-element.334), channel_id=1, source_target_pairs={{0,1},{1,2},{2,3},{3,0},{4,5},{5,6},{6,7},{7,4},{8,9},{9,10},{10,1... | collective-permute-start | bytes 393224 | tf_op jit(solution)/shard_map/while/body/eval_jaxpr/ppermute | solution.py:13
  111.4 27.1 %collective-permute-start.2 = (bf16[2,256,8,128]{1,3,2,0:T(8,128)(2,1)}, bf16[2,256,8,128]{1,3,2,0:T(8,128)(2,1)S(1)}, u32[]{:S(2)}, u32[]{:S(2)}) collective-permute-start(bf16[2,256,8,128]{1,3,2,0:T(8,128)(2,1)} %get-tuple-element.335), channel_id=1, source_target_pairs={{4,0},{8,4},{12,8},{16,12},{20,16},{24,20},{28,24},{5,1},{9,5},{13... | collective-permute-start | bytes 3145736 | tf_op jit(solution)/shard_map/while/body/eval_jaxpr/ppermute | solution.py:24
  117.6 20.9 %copy-start.1 = (f32[9,256,256]{1,2,0:T(8,128)}, f32[9,256,256]{1,2,0:T(8,128)S(1)}, u32[]{:S(2)}) copy-start(f32[9,256,256]{1,2,0:T(8,128)S(1)} %select_add_fusion.2) | copy-start | bytes 7077892 | tf_op jit(solution)/shard_map/while
  141.5 5.0 collective-permute-start
  142.6 5.6 %collective-permute-start.1 = (bf16[2,256,1,128]{1,3,2,0:T(8,128)(2,1)}, bf16[2,256,1,128]{1,3,2,0:T(8,128)(2,1)}, u32[]{:S(2)}, u32[]{:S(2)}) collective-permute-start(bf16[2,256,1,128]{1,3,2,0:T(8,128)(2,1)} %get-tuple-element.334), channel_id=1, source_target_pairs={{0,1},{1,2},{2,3},{3,0},{4,5},{5,6},{6,7},{7,4},{8,9},{9,10},{10,1... | collective-permute-start | bytes 393224 | tf_op jit(solution)/shard_map/while/body/eval_jaxpr/ppermute | solution.py:13
  152.0 27.9 %collective-permute-start.2 = (bf16[2,256,8,128]{1,3,2,0:T(8,128)(2,1)}, bf16[2,256,8,128]{1,3,2,0:T(8,128)(2,1)S(1)}, u32[]{:S(2)}, u32[]{:S(2)}) collective-permute-start(bf16[2,256,8,128]{1,3,2,0:T(8,128)(2,1)} %get-tuple-element.335), channel_id=1, source_target_pairs={{4,0},{8,4},{12,8},{16,12},{20,16},{24,20},{28,24},{5,1},{9,5},{13... | collective-permute-start | bytes 3145736 | tf_op jit(solution)/shard_map/while/body/eval_jaxpr/ppermute | solution.py:24
  158.2 21.7 %copy-start.1 = (f32[9,256,256]{1,2,0:T(8,128)}, f32[9,256,256]{1,2,0:T(8,128)S(1)}, u32[]{:S(2)}) copy-start(f32[9,256,256]{1,2,0:T(8,128)S(1)} %select_add_fusion.2) | copy-start | bytes 7077892 | tf_op jit(solution)/shard_map/while
  182.9 3.9 collective-permute-start
  183.0 5.6 %collective-permute-start.1 = (bf16[2,256,1,128]{1,3,2,0:T(8,128)(2,1)}, bf16[2,256,1,128]{1,3,2,0:T(8,128)(2,1)}, u32[]{:S(2)}, u32[]{:S(2)}) collective-permute-start(bf16[2,256,1,128]{1,3,2,0:T(8,128)(2,1)} %get-tuple-element.334), channel_id=1, source_target_pairs={{0,1},{1,2},{2,3},{3,0},{4,5},{5,6},{6,7},{7,4},{8,9},{9,10},{10,1... | collective-permute-start | bytes 393224 | tf_op jit(solution)/shard_map/while/body/eval_jaxpr/ppermute | solution.py:13
  192.4 27.1 %collective-permute-start.2 = (bf16[2,256,8,128]{1,3,2,0:T(8,128)(2,1)}, bf16[2,256,8,128]{1,3,2,0:T(8,128)(2,1)S(1)}, u32[]{:S(2)}, u32[]{:S(2)}) collective-permute-start(bf16[2,256,8,128]{1,3,2,0:T(8,128)(2,1)} %get-tuple-element.335), channel_id=1, source_target_pairs={{4,0},{8,4},{12,8},{16,12},{20,16},{24,20},{28,24},{5,1},{9,5},{13... | collective-permute-start | bytes 3145736 | tf_op jit(solution)/shard_map/while/body/eval_jaxpr/ppermute | solution.py:24
  222.5 5.1 collective-permute-start
  223.7 5.5 %collective-permute-start.1 = (bf16[2,256,1,128]{1,3,2,0:T(8,128)(2,1)}, bf16[2,256,1,128]{1,3,2,0:T(8,128)(2,1)}, u32[]{:S(2)}, u32[]{:S(2)}) collective-permute-start(bf16[2,256,1,128]{1,3,2,0:T(8,128)(2,1)} %get-tuple-element.334), channel_id=1, source_target_pairs={{0,1},{1,2},{2,3},{3,0},{4,5},{5,6},{6,7},{7,4},{8,9},{9,10},{10,1... | collective-permute-start | bytes 393224 | tf_op jit(solution)/shard_map/while/body/eval_jaxpr/ppermute | solution.py:13
  233.0 27.9 %collective-permute-start.2 = (bf16[2,256,8,128]{1,3,2,0:T(8,128)(2,1)}, bf16[2,256,8,128]{1,3,2,0:T(8,128)(2,1)S(1)}, u32[]{:S(2)}, u32[]{:S(2)}) collective-permute-start(bf16[2,256,8,128]{1,3,2,0:T(8,128)(2,1)} %get-tuple-element.335), channel_id=1, source_target_pairs={{4,0},{8,4},{12,8},{16,12},{20,16},{24,20},{28,24},{5,1},{9,5},{13... | collective-permute-start | bytes 3145736 | tf_op jit(solution)/shard_map/while/body/eval_jaxpr/ppermute | solution.py:24
  239.3 21.7 %copy-start.1 = (f32[9,256,256]{1,2,0:T(8,128)}, f32[9,256,256]{1,2,0:T(8,128)S(1)}, u32[]{:S(2)}) copy-start(f32[9,256,256]{1,2,0:T(8,128)S(1)} %select_add_fusion.2) | copy-start | bytes 7077892 | tf_op jit(solution)/shard_map/while
  263.9 3.9 collective-permute-start
  263.9 5.6 %collective-permute-start.1 = (bf16[2,256,1,128]{1,3,2,0:T(8,128)(2,1)}, bf16[2,256,1,128]{1,3,2,0:T(8,128)(2,1)}, u32[]{:S(2)}, u32[]{:S(2)}) collective-permute-start(bf16[2,256,1,128]{1,3,2,0:T(8,128)(2,1)} %get-tuple-element.334), channel_id=1, source_target_pairs={{0,1},{1,2},{2,3},{3,0},{4,5},{5,6},{6,7},{7,4},{8,9},{9,10},{10,1... | collective-permute-start | bytes 393224 | tf_op jit(solution)/shard_map/while/body/eval_jaxpr/ppermute | solution.py:13
  273.3 146.9 %collective-permute-start.2 = (bf16[2,256,8,128]{1,3,2,0:T(8,128)(2,1)}, bf16[2,256,8,128]{1,3,2,0:T(8,128)(2,1)S(1)}, u32[]{:S(2)}, u32[]{:S(2)}) collective-permute-start(bf16[2,256,8,128]{1,3,2,0:T(8,128)(2,1)} %get-tuple-element.335), channel_id=1, source_target_pairs={{4,0},{8,4},{12,8},{16,12},{20,16},{24,20},{28,24},{5,1},{9,5},{13... | collective-permute-start | bytes 3145736 | tf_op jit(solution)/shard_map/while/body/eval_jaxpr/ppermute | solution.py:24
  279.6 140.7 %copy-start.1 = (f32[9,256,256]{1,2,0:T(8,128)}, f32[9,256,256]{1,2,0:T(8,128)S(1)}, u32[]{:S(2)}) copy-start(f32[9,256,256]{1,2,0:T(8,128)S(1)} %select_add_fusion.2) | copy-start | bytes 7077892 | tf_op jit(solution)/shard_map/while
  423.3 3.8 collective-permute-start
  423.4 5.8 %collective-permute-start.1 = (bf16[2,256,1,128]{1,3,2,0:T(8,128)(2,1)}, bf16[2,256,1,128]{1,3,2,0:T(8,128)(2,1)}, u32[]{:S(2)}, u32[]{:S(2)}) collective-permute-start(bf16[2,256,1,128]{1,3,2,0:T(8,128)(2,1)} %get-tuple-element.334), channel_id=1, source_target_pairs={{0,1},{1,2},{2,3},{3,0},{4,5},{5,6},{6,7},{7,4},{8,9},{9,10},{10,1... | collective-permute-start | bytes 393224 | tf_op jit(solution)/shard_map/while/body/eval_jaxpr/ppermute | solution.py:13
  451.2 27.0 %collective-permute-start.2 = (bf16[2,256,8,128]{1,3,2,0:T(8,128)(2,1)}, bf16[2,256,8,128]{1,3,2,0:T(8,128)(2,1)S(1)}, u32[]{:S(2)}, u32[]{:S(2)}) collective-permute-start(bf16[2,256,8,128]{1,3,2,0:T(8,128)(2,1)} %get-tuple-element.335), channel_id=1, source_target_pairs={{4,0},{8,4},{12,8},{16,12},{20,16},{24,20},{28,24},{5,1},{9,5},{13... | collective-permute-start | bytes 3145736 | tf_op jit(solution)/shard_map/while/body/eval_jaxpr/ppermute | solution.py:24
  (30 other events, 140.3 us)
Sparse Core Ops, SparseCore 0:
  483.0 52.0 all-reduce.13
where the time goes:
time: 546 us; the launch traced here: 545 us
  waiting for transfers between devices  370 us (68%)
  other arithmetic  63.1 us (12%)
  local copies, waits for them, and re-layouts  55 us (10%)
  starting transfers between devices  19.4 us (4%)
  matrix products  17.4 us (3%)
  between operations  14.1 us (3%)
  loops' own time  5.84 us (1%)
    ppermute x8, waiting for transfers between devices, from_behind(): return lax.ppermute(block, axis, route)  288 us
    psum x1, waiting for transfers between devices, per_device(): weight_grad = lax.psum(kernel_acc * scale, 'tile')  49.5 us
    another operation x15, local copies, waits for them, and re-layouts  19.9 us
    add x8, other arithmetic, one_tick(): kernel_acc = kernel_acc + partial_k  19.5 us
    select_n x8, other arithmetic, one_tick(): grads = jnp.where(valid, lowered, old_grads)  19 us
    ppermute x9, waiting for transfers between devices, padded_2(): lax.ppermute(lax.slice_in_dim(block, 0, width, axis=dim), axis, backward)  18.8 us
    ppermute x9, waiting for transfers between devices, padded_2(): lax.ppermute(lax.slice_in_dim(block, block.shape[dim] - width, None, axis...  14.2 us
  transfers between devices with their start and end apart: 27, of which 25 were waited for; matrix products, arithmetic and copies ran while one was open for 9% of the time, Pallas kernels for 0%

commit v1 on v0

v1 whole, which is shorter than its diff:
```python
import functools

import jax
import jax.numpy as jnp
from jax import lax
from jax.experimental import pallas as pl
from jax.experimental.pallas import tpu as pltpu
from jax.sharding import PartitionSpec as P

MESH = pl.DeviceIdType.MESH


def shifted(value, offset):
    width = value.shape[-1]
    if offset == 0:
        return value
    lane = lax.broadcasted_iota(jnp.int32, value.shape, value.ndim - 1)
    moved = pltpu.roll(value, (-offset) % width, value.ndim - 1)
    edge = width - 1 if offset == 1 else 0
    return jnp.where(lane == edge, 0.0, moved)


def chain_kernel(
    n_section, n_tile, acts, wide, cot, grads, wgrad,
    rows_in, hidden3, slope, acts_rim, cot_rim,
    rim_send, rim_recv, main_send, main_recv, edge_send, edge_recv,
):
    batches, height, chans, width = acts.shape
    pair = 2
    blocks = height // pair
    s = lax.axis_index("section")
    t = lax.axis_index("tile")
    t_low = lax.rem(t + n_tile - 1, n_tile)
    t_high = lax.rem(t + 1, n_tile)
    s_low = lax.rem(s + n_section - 1, n_section)
    s_high = lax.rem(s + 1, n_section)
    top = s == n_section - 1

    barrier = pltpu.get_barrier_semaphore()
    friends = [(s, t_low), (s, t_high)]
    for other in (s_low, s_high):
        friends += [(other, t_low), (other, t), (other, t_high)]
    for friend in friends:
        pl.semaphore_signal(barrier, inc=1, device_id=friend, device_id_type=MESH)
    pl.semaphore_wait(barrier, len(friends))

    rims = []
    for which, (source, landing) in enumerate(((cot, cot_rim), (acts, acts_rim))):
        for side, (row, target) in enumerate(((height - 1, t_high), (0, t_low))):
            rims.append(
                pltpu.make_async_remote_copy(
                    src_ref=source.at[:, row],
                    dst_ref=landing.at[side],
                    send_sem=rim_send.at[which, side],
                    recv_sem=rim_recv.at[which, side],
                    device_id=(s, target),
                    device_id_type=MESH,
                )
            )
    for copy in rims:
        copy.start()

    def main_copy(m, block):
        return pltpu.make_async_remote_copy(
            src_ref=grads.at[m, pl.ds(block * pair, pair)],
            dst_ref=rows_in.at[m, pl.ds(block * pair + 1, pair)],
            send_sem=main_send.at[m, block],
            recv_sem=main_recv.at[m, block],
            device_id=(s_low, t),
            device_id_type=MESH,
        )

    def edge_copy(m, side):
        row, slot, target = ((height - 1, 0, t_high), (0, height + 1, t_low))[side]
        return pltpu.make_async_remote_copy(
            src_ref=grads.at[m, row],
            dst_ref=rows_in.at[m, slot],
            send_sem=edge_send.at[m, side],
            recv_sem=edge_recv.at[m, side],
            device_id=(s_low, target),
            device_id_type=MESH,
        )

    def fill_slope(index, carry):
        m, row = index // height, index % height
        value = acts[m, row].astype(jnp.float32)
        sigma = jax.nn.sigmoid(value)
        slope[m, row] = sigma * (1.0 + value * (1.0 - sigma))
        return carry

    lax.fori_loop(0, batches * height, fill_slope, 0)

    def put_hidden(m, slot, raw):
        value = raw.astype(jnp.float32)
        hidden = value * jax.nn.sigmoid(value)
        for place, offset in enumerate((-1, 0, 1)):
            hidden3[m, slot, pl.ds(place * chans, chans)] = shifted(hidden, offset).astype(
                jnp.bfloat16
            )

    def fill_hidden():
        def one(index, carry):
            m, row = index // height, index % height
            put_hidden(m, row + 1, acts[m, row])
            return carry

        lax.fori_loop(0, batches * height, one, 0)
        for m in range(batches):
            put_hidden(m, 0, acts_rim[0, m])
            put_hidden(m, height + 1, acts_rim[1, m])

    for copy in rims:
        copy.wait()

    @pl.when(top)
    def _():
        for m in range(batches):
            rows_in[m, 0] = cot_rim[0, m]
            rows_in[m, pl.ds(1, height)] = cot[m]
            rows_in[m, height + 1] = cot_rim[1, m]

    @pl.when(jnp.logical_not(top))
    def _():
        fill_hidden()

    wgrad[...] = jnp.zeros_like(wgrad)

    def one_batch(m, carry):
        @pl.when(jnp.logical_not(top))
        def _():
            for side in range(2):
                edge_copy(m, side).wait_recv()
            for block in range(blocks):
                main_copy(m, block).wait_recv()

        def one_block(block, inner):
            first = block * pair
            right = jnp.concatenate(
                [
                    rows_in[m, pl.ds(first + j, 3)].reshape(3 * chans, width)
                    for j in range(pair)
                ],
                axis=1,
            )
            product = jnp.dot(wide[...], right, preferred_element_type=jnp.float32)
            for j in range(pair):
                part = product[:, j * width : (j + 1) * width]
                back = part[chans : 2 * chans]
                back = back + shifted(part[:chans], 1)
                back = back + shifted(part[2 * chans :], -1)
                row = first + j
                upper = rows_in[m, row + 1].astype(jnp.float32)
                grads[m, row] = (upper + back * slope[m, row]).astype(jnp.bfloat16)

            @pl.when(s > 0)
            def _():
                main_copy(m, block).start()

                @pl.when(block == 0)
                def _():
                    edge_copy(m, 1).start()

                @pl.when(block == blocks - 1)
                def _():
                    edge_copy(m, 0).start()

            return inner

        lax.fori_loop(0, blocks, one_block, 0)

        @pl.when(jnp.logical_and(top, m == 0))
        def _():
            fill_hidden()

        left = jnp.concatenate([rows_in[m, 1 + row] for row in range(height)], axis=1)

        def one_offset(a, inner):
            seen = jnp.concatenate([hidden3[m, a + row] for row in range(height)], axis=1)
            product = lax.dot_general(
                left, seen, (((1,), (1,)), ((), ())), preferred_element_type=jnp.float32
            )
            for place in range(3):
                wgrad[3 * a + place] += product[:, place * chans : (place + 1) * chans]
            return inner

        lax.fori_loop(0, 3, one_offset, 0)
        return carry

    lax.fori_loop(0, batches, one_batch, 0)

    @pl.when(s > 0)
    def _():
        for m in range(batches):
            for side in range(2):
                edge_copy(m, side).wait_send()
            for block in range(blocks):
                main_copy(m, block).wait_send()


def per_device(acts, weights, cotangent):
    n_section = lax.axis_size("section")
    n_tile = lax.axis_size("tile")
    batches, chans, height, width = acts.shape[1:]
    rows_first = jnp.transpose(acts[0], (0, 2, 1, 3))
    cot_rows = jnp.transpose(cotangent, (0, 2, 1, 3))
    wide = weights[0].reshape(3, 3, chans, chans)[::-1]
    wide = jnp.transpose(wide, (1, 3, 0, 2)).reshape(3 * chans, 3 * chans)
    scale = 1.0 / jnp.sqrt(jnp.float32(batches * height * n_tile * width))

    vmem = pl.BlockSpec(memory_space=pltpu.VMEM)
    grads, wgrad = pl.pallas_call(
        functools.partial(chain_kernel, n_section, n_tile),
        out_shape=(
            jax.ShapeDtypeStruct((batches, height, chans, width), jnp.bfloat16),
            jax.ShapeDtypeStruct((9, chans, chans), jnp.float32),
        ),
        in_specs=[vmem] * 3,
        out_specs=(vmem, vmem),
        scratch_shapes=[
            pltpu.VMEM((batches, height + 2, chans, width), jnp.bfloat16),
            pltpu.VMEM((batches, height + 2, 3 * chans, width), jnp.bfloat16),
            pltpu.VMEM((batches, height, chans, width), jnp.float32),
            pltpu.VMEM((2, batches, chans, width), jnp.bfloat16),
            pltpu.VMEM((2, batches, chans, width), jnp.bfloat16),
            pltpu.SemaphoreType.DMA((2, 2)),
            pltpu.SemaphoreType.DMA((2, 2)),
            pltpu.SemaphoreType.DMA((batches, height // 2)),
            pltpu.SemaphoreType.DMA((batches, height // 2)),
            pltpu.SemaphoreType.DMA((batches, 2)),
            pltpu.SemaphoreType.DMA((batches, 2)),
        ],
        compiler_params=pltpu.CompilerParams(
            collective_id=0, has_side_effects=True, vmem_limit_bytes=48 * 1024 * 1024
        ),
    )(rows_first, wide, cot_rows)
    weight_grad = lax.psum(wgrad * scale, "tile")
    return (jnp.transpose(grads, (0, 2, 1, 3))[None], weight_grad[None])


def solution(mesh):
    placed = (
        P("section", None, None, "tile", None),
        P("section", None, None, None),
        P(None, None, "tile", None),
    )
    return jax.shard_map(
        per_device,
        mesh=mesh,
        in_specs=placed,
        out_specs=(P("section", None, None, "tile", None), P("section", None, None, None)),
        check_vma=False,
    )
```

time: 546 us -> 240 us (0.44)
  waiting for transfers between devices: 370 us -> 51.1 us
  Pallas kernels: 0 us -> 150 us
  other arithmetic: 63.1 us -> 3.27 us
  local copies, waits for them, and re-layouts: 55 us -> 20.9 us
  starting transfers between devices: 19.4 us -> 0.04 us
  matrix products: 17.4 us -> 0 us
  loops' own time: 5.84 us -> 0 us
    ppermute x26 -> x0, waiting for transfers between devices: 321 us -> none  [the longest x8 288 us: from_behind(): return lax.ppermute(block, axis, route)]
    pallas_call x0 -> x1, Pallas kernels: none -> 150 us  [per_device(): pl.pallas_call(functools.partial(chain_kernel, n_section, n_tile), out_sh...]
    select_n x16 -> x0, other arithmetic: 29.7 us -> none  [the longest x8 19 us: one_tick(): grads = jnp.where(valid, lowered, old_grads)]
    add x8 -> x0, other arithmetic: 19.5 us -> none  [one_tick(): kernel_acc = kernel_acc + partial_k]
    ppermute x26 -> x0, starting transfers between devices: 19.3 us -> none  [the longest x8 10.2 us: from_behind(): return lax.ppermute(block, axis, route)]
    dot_general x18 -> x0, matrix products: 17.4 us -> none  [the longest x9 10.6 us: kernel_grad(): jnp.einsum('gorc,girc->oi', grad_mid, seen, preferred_element_type=jnp.fl...]
    another operation x15 -> x1, local copies, waits for them, and re-layouts: 19.9 us -> 3.59 us  [per_device(): wide = weights[0].reshape(3, 3, chans, chans)[::-1]]
    while x66 -> x0, local copies, waits for them, and re-layouts: 12.3 us -> none
  transfers between devices with their start and end apart: 27 -> 1, of which waited for: 25 -> 1; matrix products, arithmetic and copies ran while one was open for 9% -> 1% of each run, Pallas kernels for 0% -> 0%
where the time goes in v1:
time: 240 us; the launch traced here: 239 us
  Pallas kernels  150 us (62%)
  waiting for transfers between devices  51.1 us (21%)
  local copies, waits for them, and re-layouts  20.9 us (9%)
  between operations  14.1 us (6%)
  other arithmetic  3.27 us (1%)
    pallas_call x1, Pallas kernels, per_device(): pl.pallas_call(functools.partial(chain_kernel, n_section, n_tile), out_sh...  150 us
    psum x1, waiting for transfers between devices, per_device(): weight_grad = lax.psum(wgrad * scale, 'tile')  51.1 us
    rev x1, local copies, waits for them, and re-layouts, per_device(): wide = weights[0].reshape(3, 3, chans, chans)[::-1]  9.07 us
    unnamed x7, local copies, waits for them, and re-layouts  8.23 us
  transfers between devices with their start and end apart: 1, of which 1 were waited for; matrix products, arithmetic and copies ran while one was open for 1% of the time, Pallas kernels for 0%

profile of v1, /device:TPU:0, one launch (start us, length us, event | category | flops | bytes accessed | tf_op | source)
XLA Modules:
  0.0 239.1 jit_solution(6747424574960656634)
XLA Ops:
  7.2 0.0 copy-start
  7.2 0.0 all-reduce.2.cloned.1.call-start
  7.2 1.5 copy.17
  8.7 0.0 copy-done
  8.7 0.2 copy.16
  8.9 3.6 %copy.10 = bf16[3,3,256,256]{2,0,3,1:T(4,128)(2,1)} copy(bf16[3,3,256,256]{3,2,1,0:T(8,128)(2,1)} %bitcast.23) | data formatting | bytes 2359296 | tf_op jit(solution)/shard_map/reshape;squeeze | solution.py:206
  12.5 9.1 %rev.3 = bf16[3,3,256,256]{2,0,3,1:T(4,128)(2,1)} reverse(bf16[3,3,256,256]{2,0,3,1:T(4,128)(2,1)} %copy.10), dimensions={0} | reverse | bytes 2359296 | tf_op jit(solution)/shard_map/rev | solution.py:206
  21.6 1.7 copy.13
  23.3 149.7 %shard_map.50 = (bf16[2,8,256,128]{3,2,1,0:T(8,128)(2,1)S(1)}, f32[9,256,256]{2,1,0:T(8,128)}) custom-call(bf16[2,8,256,128]{3,2,1,0:T(8,128)(2,1)S(1)} %bitcast.19, bf16[768,768]{1,0:T(8,128)(2,1)S(1)} %bitcast.18, bf16[2,8,256,128]{3,2,1,0:T(8,128)(2,1)S(1)} %bitcast.20), custom_call_target="tpu_custom_call" | custom-call | tf_op jit(solution)/shard_map/pallas_call | solution.py:211
  173.0 3.3 %multiply_bitcast_fusion = f32[1,9,256,256]{3,2,1,0:T(8,128)} fusion(f32[9,256,256]{2,1,0:T(8,128)} %get-tuple-element.5), kind=kLoop, calls=%fused_computation | loop fusion | flops 589824 | bytes 4718592 | tf_op jit(solution)/shard_map/broadcast_in_dim | solution.py:237
  176.3 0.0 all-reduce.2.cloned.1.call-update
  176.3 1.6 copy.12
  177.9 51.1 %all-reduce.2.cloned.1.call-done = f32[1,9,256,256]{3,2,1,0:T(8,128)} async-done(((f32[1,9,256,256]{3,2,1,0:T(8,128)}), f32[1,9,256,256]{3,2,1,0:T(8,128)}) %all-reduce.2.cloned.1.call-update) | async-done | bytes 2359312 | tf_op jit(solution)/shard_map/psum | solution.py:236
  229.0 3.2 %copy.19 = f32[1,9,256,256]{3,2,1,0:T(8,128)} copy(f32[1,9,256,256]{3,2,1,0:T(8,128)} %all-reduce.2.cloned.1.call-done) | data formatting | bytes 4718592
Async XLA Ops:
  7.2 1.6 copy-start
  7.2 221.9 %all-reduce.2.cloned.1.call-start = ((), (), s32[]{:S(2)}) async-start(), calls=%async_computation | async-start | bytes 4718592 | tf_op jit(solution)/shard_map/psum | solution.py:236
Sparse Core Ops, SparseCore 0:
  176.4 52.5 all-reduce.1

commit v2 on v1

--- a/solution.py
+++ b/solution.py
@@ -1,4 +1,5 @@
 import functools
+import math
 
 import jax
 import jax.numpy as jnp
@@ -21,9 +22,11 @@
 
 
 def chain_kernel(
-    n_section, n_tile, acts, wide, cot, grads, wgrad,
+    n_section, n_tile, scale, acts, wide, cot, grads, wgrad,
     rows_in, hidden3, slope, acts_rim, cot_rim,
+    parts, landed, final,
     rim_send, rim_recv, main_send, main_recv, edge_send, edge_recv,
+    part_send, part_recv, whole_send, whole_recv,
 ):
     batches, height, chans, width = acts.shape
     pair = 2
@@ -37,7 +40,7 @@
     top = s == n_section - 1
 
     barrier = pltpu.get_barrier_semaphore()
-    friends = [(s, t_low), (s, t_high)]
+    friends = [(s, lax.rem(t + step, n_tile)) for step in range(1, n_tile)]
     for other in (s_low, s_high):
         friends += [(other, t_low), (other, t), (other, t_high)]
     for friend in friends:
@@ -126,18 +129,25 @@
     wgrad[...] = jnp.zeros_like(wgrad)
 
     def one_batch(m, carry):
-        @pl.when(jnp.logical_not(top))
-        def _():
-            for side in range(2):
-                edge_copy(m, side).wait_recv()
-            for block in range(blocks):
-                main_copy(m, block).wait_recv()
-
-        def one_block(block, inner):
+        def one_block(step, inner):
+            block = (3 * step) % 5 - 2 * (step // 3)
+
+            @pl.when(jnp.logical_and(jnp.logical_not(top), step == 0))
+            def _():
+                main_copy(m, 0).wait_recv()
+                edge_copy(m, 0).wait_recv()
+                main_copy(m, 1).wait_recv()
+
+            @pl.when(jnp.logical_and(jnp.logical_not(top), step == 1))
+            def _():
+                main_copy(m, 3).wait_recv()
+                edge_copy(m, 1).wait_recv()
+                main_copy(m, 2).wait_recv()
+
             first = block * pair
             right = jnp.concatenate(
                 [
-                    rows_in[m, pl.ds(first + j, 3)].reshape(3 * chans, width)
+                    jnp.concatenate([rows_in[m, first + j + k] for k in (2, 1, 0)], axis=0)
                     for j in range(pair)
                 ],
                 axis=1,
@@ -156,11 +166,11 @@
             def _():
                 main_copy(m, block).start()
 
-                @pl.when(block == 0)
+                @pl.when(step == 0)
                 def _():
                     edge_copy(m, 1).start()
 
-                @pl.when(block == blocks - 1)
+                @pl.when(step == 1)
                 def _():
                     edge_copy(m, 0).start()
 
@@ -180,13 +190,71 @@
                 left, seen, (((1,), (1,)), ((), ())), preferred_element_type=jnp.float32
             )
             for place in range(3):
-                wgrad[3 * a + place] += product[:, place * chans : (place + 1) * chans]
+                rows = pl.ds(pl.multiple_of((3 * a + place) * chans, chans), chans)
+                wgrad[rows] += product[:, place * chans : (place + 1) * chans]
             return inner
 
         lax.fori_loop(0, 3, one_offset, 0)
         return carry
 
     lax.fori_loop(0, batches, one_batch, 0)
+
+    share = wgrad.shape[0] // n_tile
+
+    def rows_of(tile):
+        return pl.ds(pl.multiple_of(tile * share, share), share)
+
+    def round_part(k, carry):
+        rows = pl.ds(pl.multiple_of(k * chans, chans), chans)
+        parts[rows] = wgrad[rows].astype(jnp.bfloat16)
+        return carry
+
+    lax.fori_loop(0, 9, round_part, 0)
+    sends = []
+    for step in range(1, n_tile):
+        other = lax.rem(t + step, n_tile)
+        sends.append(
+            pltpu.make_async_remote_copy(
+                src_ref=parts.at[rows_of(other)],
+                dst_ref=landed.at[step - 1],
+                send_sem=part_send.at[step - 1],
+                recv_sem=part_recv.at[step - 1],
+                device_id=(s, other),
+                device_id_type=MESH,
+            )
+        )
+    for copy in sends:
+        copy.start()
+    total = wgrad[rows_of(t)]
+    for step, copy in enumerate(sends):
+        copy.wait_recv()
+        total = total + landed[step].astype(jnp.float32)
+    final[rows_of(t)] = (total * scale).astype(jnp.bfloat16)
+    wholes = []
+    for step in range(1, n_tile):
+        wholes.append(
+            pltpu.make_async_remote_copy(
+                src_ref=final.at[rows_of(t)],
+                dst_ref=final.at[rows_of(t)],
+                send_sem=whole_send.at[step - 1],
+                recv_sem=whole_recv.at[step - 1],
+                device_id=(s, lax.rem(t + step, n_tile)),
+                device_id_type=MESH,
+            )
+        )
+    for copy in wholes:
+        copy.start()
+    for copy in sends:
+        copy.wait_send()
+    for copy in wholes:
+        copy.wait()
+
+    def widen(k, carry):
+        rows = pl.ds(pl.multiple_of(k * chans, chans), chans)
+        wgrad[rows] = final[rows].astype(jnp.float32)
+        return carry
+
+    lax.fori_loop(0, 9, widen, 0)
 
     @pl.when(s > 0)
     def _():
@@ -203,16 +271,17 @@
     batches, chans, height, width = acts.shape[1:]
     rows_first = jnp.transpose(acts[0], (0, 2, 1, 3))
     cot_rows = jnp.transpose(cotangent, (0, 2, 1, 3))
-    wide = weights[0].reshape(3, 3, chans, chans)[::-1]
+    wide = weights[0].reshape(3, 3, chans, chans)
     wide = jnp.transpose(wide, (1, 3, 0, 2)).reshape(3 * chans, 3 * chans)
-    scale = 1.0 / jnp.sqrt(jnp.float32(batches * height * n_tile * width))
+    scale = 1.0 / math.sqrt(batches * height * n_tile * width)
+    taps = 9 * chans
 
     vmem = pl.BlockSpec(memory_space=pltpu.VMEM)
     grads, wgrad = pl.pallas_call(
-        functools.partial(chain_kernel, n_section, n_tile),
+        functools.partial(chain_kernel, n_section, n_tile, scale),
         out_shape=(
             jax.ShapeDtypeStruct((batches, height, chans, width), jnp.bfloat16),
-            jax.ShapeDtypeStruct((9, chans, chans), jnp.float32),
+            jax.ShapeDtypeStruct((taps, chans), jnp.float32),
         ),
         in_specs=[vmem] * 3,
         out_specs=(vmem, vmem),
@@ -222,18 +291,22 @@
             pltpu.VMEM((batches, height, chans, width), jnp.float32),
             pltpu.VMEM((2, batches, chans, width), jnp.bfloat16),
             pltpu.VMEM((2, batches, chans, width), jnp.bfloat16),
+            pltpu.VMEM((taps, chans), jnp.bfloat16),
+            pltpu.VMEM((n_tile - 1, taps // n_tile, chans), jnp.bfloat16),
+            pltpu.VMEM((taps, chans), jnp.bfloat16),
             pltpu.SemaphoreType.DMA((2, 2)),
             pltpu.SemaphoreType.DMA((2, 2)),
             pltpu.SemaphoreType.DMA((batches, height // 2)),
             pltpu.SemaphoreType.DMA((batches, height // 2)),
             pltpu.SemaphoreType.DMA((batches, 2)),
             pltpu.SemaphoreType.DMA((batches, 2)),
-        ],
+        ]
+        + [pltpu.SemaphoreType.DMA((n_tile - 1,))] * 4,
         compiler_params=pltpu.CompilerParams(
             collective_id=0, has_side_effects=True, vmem_limit_bytes=48 * 1024 * 1024
         ),
     )(rows_first, wide, cot_rows)
-    weight_grad = lax.psum(wgrad * scale, "tile")
+    weight_grad = wgrad.reshape(9, chans, chans)
     return (jnp.transpose(grads, (0, 2, 1, 3))[None], weight_grad[None])
 
 

time: 240 us -> 169 us (0.70)
  waiting for transfers between devices: 51.1 us -> 0 us
  between operations: 14.1 us -> 0.67 us
  local copies, waits for them, and re-layouts: 20.9 us -> 11.5 us
  Pallas kernels: 150 us -> 154 us
  other arithmetic: 3.27 us -> 0 us
    psum x1 -> x0, waiting for transfers between devices: 51.1 us -> none  [per_device(): weight_grad = lax.psum(wgrad * scale, 'tile')]
    rev x1 -> x0, local copies, waits for them, and re-layouts: 9.07 us -> none  [per_device(): wide = weights[0].reshape(3, 3, chans, chans)[::-1]]
    pallas_call x1, Pallas kernels: 150 us -> 154 us  [per_device(): pl.pallas_call(functools.partial(chain_kernel, n_section, n_tile, scale),...]
    broadcast_in_dim x1 -> x0, other arithmetic: 3.27 us -> none  [per_device(): return (jnp.transpose(grads, (0, 2, 1, 3))[None], weight_grad[None])]
    unnamed x7 -> x9, local copies, waits for them, and re-layouts: 8.23 us -> 9.31 us
  transfers between devices with their start and end apart: 1 -> 0, of which waited for: 1 -> 0; matrix products, arithmetic and copies ran while one was open for 1% -> 0% of each run, Pallas kernels for 0% -> 0%
where the time goes in v2:
time: 169 us; the launch traced here: 166 us
  Pallas kernels  154 us (91%)
  local copies, waits for them, and re-layouts  11.5 us (7%)
    pallas_call x1, Pallas kernels, per_device(): pl.pallas_call(functools.partial(chain_kernel, n_section, n_tile, scale),...  154 us
    unnamed x9, local copies, waits for them, and re-layouts  9.31 us

profile of v2, /device:TPU:0, one launch (start us, length us, event | category | flops | bytes accessed | tf_op | source)
XLA Modules:
  0.0 166.5 jit_solution(3662748190061490786)
XLA Ops:
  0.6 0.0 copy-start.1
  0.6 1.5 copy.17
  2.1 0.0 copy-start
  2.2 0.0 copy-done.1
  2.2 0.2 copy.16
  2.4 1.1 copy-done
  3.4 2.2 %copy.10 = bf16[3,3,256,256]{2,0,3,1:T(4,128)(2,1)} copy(bf16[3,3,256,256]{3,2,1,0:T(8,128)(2,1)S(1)} %bitcast.23) | data formatting | bytes 2359296 | tf_op jit(solution)/shard_map/reshape;squeeze | solution.py:274
  5.6 1.7 %copy.13 = bf16[96,8,3,256]{3,1,2,0:T(8,128)(2,1)S(1)} copy(bf16[96,8,3,256]{3,2,1,0:T(4,128)(2,1)} %bitcast.21) | data formatting | bytes 2359296
  7.3 154.3 %shard_map.50 = (bf16[2,8,256,128]{3,2,1,0:T(8,128)(2,1)S(1)}, f32[2304,256]{1,0:T(8,128)}) custom-call(bf16[2,8,256,128]{3,2,1,0:T(8,128)(2,1)S(1)} %bitcast.18, bf16[768,768]{1,0:T(8,128)(2,1)S(1)} %bitcast.17, bf16[2,8,256,128]{3,2,1,0:T(8,128)(2,1)S(1)} %bitcast.19), custom_call_target="tpu_custom_call" | custom-call | tf_op jit(solution)/shard_map/pallas_call | solution.py:280
  161.6 1.6 copy.12
  163.2 3.2 %copy.19 = f32[1,9,256,256]{3,2,1,0:T(8,128)} copy(f32[1,9,256,256]{3,2,1,0:T(8,128)} %bitcast.22) | data formatting | bytes 4718592
Async XLA Ops:
  0.6 1.5 copy-start.1
  2.1 1.3 copy-start
